TPU v7x, 256 devices: a whole 4x4x8 slice. The times are simulated.
256 devices in a mesh: slab: 32 (over x, z), col: 4 (over y), pb: 2 (over core).
Axes of the slice: x: 4, y: 4, z: 8, core: 2. Of those that a mesh axis runs over, the one named last changes fastest.
Arguments:
- queries_raw: float32 [1024, 768], P(('slab', 'col', 'pb')), may hold values from -1.5 to 1.5
- projection: float32 [768, 768], replicated, may hold values from -0.21875 to 0.21875
- passages: bfloat16 [524288, 768], P(('slab', 'col')), may hold values from -17 to 17
- positives: int32 [1024, 4], P(('slab', 'col', 'pb')), may hold values from 0 to 524287
Outputs:
- loss: float32 [1024], P(('slab', 'col', 'pb'))
- grad_raw: float32 [1024, 768], P(('slab', 'col', 'pb'))
- grad_projection: float32 [768, 768], replicated
All inputs are finite; a program needn't handle non-finite values.
Results may differ from a plain program's by a relative error of at most 0.0053.
Values may be sent and summed in bfloat16 or wider, within the bound.
No kernel may reach another device: no remote copies, remote signals or barrier semaphores. Data moves between devices by JAX's collectives and lax.ppermute only.
A program may use at most 128 MiB of HBM per device.

v0:
```python
import jax
import jax.numpy as jnp
from jax import lax
from jax.sharding import PartitionSpec as P

POS = 4


def shards(queries_raw, projection, passages, positives):
    hp = lax.Precision.HIGHEST
    local_rows = passages.shape[0]
    own_queries = queries_raw.shape[0]
    group = lax.axis_size(("slab", "col"))
    scale = 1.0 / (4.0 * local_rows * group)
    projected = jnp.dot(queries_raw, projection, precision=hp, preferred_element_type=jnp.float32)
    query_emb = projected.astype(jnp.bfloat16)
    all_emb, all_pos = (
        lax.all_gather(query_emb, ("slab", "col"), axis=0, tiled=True),
        lax.all_gather(positives, ("slab", "col"), axis=0, tiled=True),
    )
    offset = lax.axis_index(("slab", "col")) * local_rows
    scores = lax.dot_general(
        all_emb, passages, (((1,), (1,)), ((), ())), preferred_element_type=jnp.float32
    )
    columns = jnp.arange(local_rows, dtype=jnp.int32)[None, :]
    local_pos = all_pos - offset
    owned = [local_pos[:, slot : slot + 1] == columns for slot in range(POS)]
    partial_pos = jnp.stack(
        [jnp.sum(jnp.where(owned[slot], scores, 0.0), axis=1) for slot in range(POS)], axis=1
    )
    pos_scores = lax.psum(partial_pos, ("slab", "col"))
    loss_part = jnp.zeros((scores.shape[0],), jnp.float32)
    slope_sum = jnp.zeros_like(scores)
    pos_list = []
    for slot in range(POS):
        sig = jax.nn.sigmoid(scores - pos_scores[:, slot : slot + 1])
        loss_part = loss_part + jnp.sum(sig, axis=1)
        slope = sig * (1.0 - sig)
        slope_sum = slope_sum + slope
        pos_list.append(-jnp.sum(slope, axis=1))
    pos_part = jnp.stack(pos_list, axis=1) * scale
    pos_grad, loss_total = lax.psum((pos_part, loss_part * scale), ("slab", "col"))
    grad = slope_sum * scale
    for slot in range(POS):
        grad = grad + jnp.where(owned[slot], pos_grad[:, slot : slot + 1], 0.0)
    grad_b = grad.astype(jnp.bfloat16)
    home = lax.axis_index(("slab", "col")) * own_queries
    summed = lax.psum(
        jnp.dot(grad_b, passages, preferred_element_type=jnp.float32), ("slab", "col")
    )
    query_grad = lax.dynamic_slice_in_dim(summed, home, own_queries, 0)
    loss = lax.dynamic_slice_in_dim(loss_total, home, own_queries, 0)
    grad_raw = jnp.dot(query_grad, projection.T, precision=hp, preferred_element_type=jnp.float32)
    term = jnp.dot(queries_raw.T, query_grad, precision=hp, preferred_element_type=jnp.float32)
    grad_projection = lax.psum(term, ("slab", "col", "pb"))
    return (loss, grad_raw, grad_projection)


def solution(mesh):
    in_specs = (
        P(("slab", "col", "pb"), None),
        P(),
        P(("slab", "col"), None),
        P(("slab", "col", "pb"), None),
    )
    out_specs = (P(("slab", "col", "pb")), P(("slab", "col", "pb"), None), P())
    return jax.shard_map(shards, mesh=mesh, in_specs=in_specs, out_specs=out_specs, check_vma=False)
```

profile of v0, /device:TPU:2, one launch (start us, length us, event | category | flops | bytes accessed | tf_op | source)
XLA Modules:
  0.0 2272.7 jit_solution(6751082720767750001)
XLA Ops:
  7.2 0.0 copy-start
  7.2 0.0 all-reduce.4.cloned.1.call-start
  7.2 309.0 %all-gather.1 = s32[128,4,4]{2,1,0:T(4,128)S(1)} all-gather(s32[1,4,4]{2,1,0:T(4,128)} %bitcast.45), channel_id=1, replica_groups=mesh['slab'=32,'col'=4,'pb'=2] {'slab','col'}, dimensions={0}, use_global_device_ids=true | all-gather | bytes 8256 | tf_op jit(solution)/shard_map/all_gather | solution.py:19
  316.2 0.0 copy-done
  316.2 1.9 fusion.5
  318.1 305.6 %all-gather = bf16[128,4,768]{2,1,0:T(4,128)(2,1)S(1)} all-gather(bf16[1,4,768]{2,1,0:T(4,128)(2,1)S(1)} %fusion.5), channel_id=1, replica_groups=mesh['slab'=32,'col'=4,'pb'=2] {'slab','col'}, dimensions={0}, use_global_device_ids=true | all-gather | bytes 792576 | tf_op jit(solution)/shard_map/all_gather | solution.py:18
  623.7 1.1 reshape.39
  624.8 0.3 fusion.14
  625.1 0.1 copy.19
  625.2 0.1 copy.20
  625.3 0.1 copy.18
  625.4 0.1 copy.21
  625.6 11.6 select_reduce_fusion.3
  637.2 348.3 %psum.35 = f32[512,4]{0,1:T(4,128)S(1)} all-reduce(f32[512,4]{0,1:T(4,128)S(1)} %pad_maximum_fusion), channel_id=1, replica_groups=mesh['slab'=32,'col'=4,'pb'=2] {'slab','col'}, use_global_device_ids=true, to_apply=%region_4.5 | all-reduce | flops 2048 | bytes 16384 | tf_op jit(solution)/shard_map/psum | solution.py:31
  985.5 17.1 fusion.1
  1002.7 681.8 %all-reduce = (f32[512]{0:T(512)S(1)}, f32[512,4]{0,1:T(4,128)S(1)}) all-reduce(f32[512]{0:T(512)S(1)} %add_multiply_fusion, f32[512,4]{0,1:T(4,128)S(1)} %maximum_multiply_fusion), channel_id=1, replica_groups=mesh['slab'=32,'col'=4,'pb'=2] {'slab','col'}, use_global_device_ids=true, to_apply=%region_9.10 | all-reduce | flops 2560 | bytes 20480 | tf_op jit(solution)/shard_map/psum | solution.py:42
  1684.5 0.0 copy-start.1
  1684.5 21.1 fusion.4
  1705.6 0.0 all-reduce.4.cloned.1.call-update
  1705.7 0.0 all-reduce.6.cloned.1.call-start
  1705.7 291.5 %all-reduce.4.cloned.1.call-done = f32[512,768]{1,0:T(8,128)} async-done(((f32[512,768]{1,0:T(8,128)}), f32[512,768]{1,0:T(8,128)}) %all-reduce.4.cloned.1.call-update) | async-done | bytes 1572880 | tf_op jit(solution)/shard_map/psum | solution.py:48
  1997.2 0.0 copy-done.1
  1997.2 4.2 convolution_bitcast_fusion
  2001.4 0.0 all-reduce.6.cloned.1.call-update
  2001.4 0.6 dynamic_slice.6
  2002.0 3.4 fusion.7
  2005.4 257.4 %all-reduce.6.cloned.1.call-done = f32[768,768]{0,1:T(8,128)} async-done(((f32[768,768]{0,1:T(8,128)}), f32[768,768]{0,1:T(8,128)}) %all-reduce.6.cloned.1.call-update) | async-done | bytes 2359312 | tf_op jit(solution)/shard_map/psum | solution.py:55
  2262.8 3.0 copy.17
  (10 shorter events, 0.1 us)
Async XLA Ops:
  7.2 309.0 %copy-start = (f32[768,768]{1,0:T(8,128)S(1)}, f32[768,768]{1,0:T(8,128)}, u32[]{:S(2)}) copy-start(f32[768,768]{1,0:T(8,128)} %param.5) | copy-start | bytes 7077892
  7.2 1990.0 %all-reduce.4.cloned.1.call-start = ((), (), s32[]{:S(2)}) async-start(), calls=%async_computation | async-start | bytes 3145728 | tf_op jit(solution)/shard_map/psum | solution.py:48
  1684.5 312.7 %copy-start.1 = (f32[4,768]{1,0:T(4,128)S(1)}, f32[4,768]{1,0:T(4,128)}, u32[]{:S(2)}) copy-start(f32[4,768]{1,0:T(4,128)} %param.4) | copy-start | bytes 36868
  1705.7 557.1 %all-reduce.6.cloned.1.call-start = ((), (), s32[]{:S(2)}) async-start(), calls=%async_computation.1 | async-start | bytes 4718592 | tf_op jit(solution)/shard_map/psum | solution.py:55
Sparse Core Ops, SparseCore 0:
  1705.8 291.3 all-reduce.3
  2004.1 258.6 all-reduce.5
where the time goes:
time: 2270 us
  blocking collectives  1640 us (72%)
  waiting for transfers between devices  549 us (24%)
  matrix products  42.2 us (2%)
    psum x1, blocking collectives, shards(): lax.psum((pos_part, loss_part * scale), ('slab', 'col'))  682 us
    psum x1, blocking collectives, shards(): pos_scores = lax.psum(partial_pos, ('slab', 'col'))  348 us
    all_gather x1, blocking collectives, shards(): lax.all_gather(positives, ('slab', 'col'), axis=0, tiled=True)  309 us
    all_gather x1, blocking collectives, shards(): lax.all_gather(query_emb, ('slab', 'col'), axis=0, tiled=True)  306 us
    psum x1, waiting for transfers between devices, shards(): lax.psum(jnp.dot(grad_b, passages, preferred_element_type=jnp.float32), (...  291 us
    psum x1, waiting for transfers between devices, shards(): grad_projection = lax.psum(term, ('slab', 'col', 'pb'))  257 us
  transfers between devices with their start and end apart: 2, of which 2 were waited for; matrix products, arithmetic and copies ran while one was open for 0% of the time, Pallas kernels for 0%

commit v1 on v0

--- a/solution.py
+++ b/solution.py
@@ -4,6 +4,12 @@
 from jax.sharding import PartitionSpec as P
 
 POS = 4
+
+
+def step_on_entries(arr_in):
+    for u in ("slab", ("col", "pb")):
+        arr_in = lax.psum(arr_in, u)
+    return arr_in
 
 
 def shards(queries_raw, projection, passages, positives):
@@ -52,7 +58,7 @@
     loss = lax.dynamic_slice_in_dim(loss_total, home, own_queries, 0)
     grad_raw = jnp.dot(query_grad, projection.T, precision=hp, preferred_element_type=jnp.float32)
     term = jnp.dot(queries_raw.T, query_grad, precision=hp, preferred_element_type=jnp.float32)
-    grad_projection = lax.psum(term, ("slab", "col", "pb"))
+    grad_projection = step_on_entries(term)
     return (loss, grad_raw, grad_projection)
 
 

time: 2270 us -> 2240 us (0.987)
  waiting for transfers between devices: 549 us -> 511 us
    psum x1 -> x2, waiting for transfers between devices: 257 us -> 220 us  [step_on_entries(): arr_in = lax.psum(arr_in, u)]
  transfers between devices with their start and end apart: 2 -> 3, of which waited for: 2 -> 3; matrix products, arithmetic and copies ran while one was open for 0% -> 0% of each run, Pallas kernels for 0% -> 0%
where the time goes in v1:
time: 2240 us; the launch traced here: 2230 us
  blocking collectives  1640 us (73%)
  waiting for transfers between devices  511 us (23%)
  matrix products  42.2 us (2%)
    psum x1, blocking collectives, shards(): lax.psum((pos_part, loss_part * scale), ('slab', 'col'))  682 us
    psum x1, blocking collectives, shards(): pos_scores = lax.psum(partial_pos, ('slab', 'col'))  348 us
    all_gather x1, blocking collectives, shards(): lax.all_gather(positives, ('slab', 'col'), axis=0, tiled=True)  309 us
    all_gather x1, blocking collectives, shards(): lax.all_gather(query_emb, ('slab', 'col'), axis=0, tiled=True)  306 us
    psum x1, waiting for transfers between devices, shards(): lax.psum(jnp.dot(grad_b, passages, preferred_element_type=jnp.float32), (...  291 us
    psum x2, waiting for transfers between devices, step_on_entries(): arr_in = lax.psum(arr_in, u)  220 us
  transfers between devices with their start and end apart: 3, of which 3 were waited for; matrix products, arithmetic and copies ran while one was open for 0% of the time, Pallas kernels for 0%

profile of v1, /device:TPU:2, one launch (start us, length us, event | category | flops | bytes accessed | tf_op | source)
XLA Modules:
  0.0 2234.9 jit_solution(16618343698675075239)
XLA Ops:
  7.2 0.0 copy-start
  7.2 0.0 all-reduce.5.cloned.1.call-start
  7.2 309.0 %all-gather.1 = s32[128,4,4]{2,1,0:T(4,128)S(1)} all-gather(s32[1,4,4]{2,1,0:T(4,128)} %bitcast.45), channel_id=1, replica_groups=mesh['slab'=32,'col'=4,'pb'=2] {'slab','col'}, dimensions={0}, use_global_device_ids=true | all-gather | bytes 8256 | tf_op jit(solution)/shard_map/all_gather | solution.py:25
  316.2 0.0 copy-done
  316.2 1.9 fusion.5
  318.1 305.6 %all-gather = bf16[128,4,768]{2,1,0:T(4,128)(2,1)S(1)} all-gather(bf16[1,4,768]{2,1,0:T(4,128)(2,1)S(1)} %fusion.5), channel_id=1, replica_groups=mesh['slab'=32,'col'=4,'pb'=2] {'slab','col'}, dimensions={0}, use_global_device_ids=true | all-gather | bytes 792576 | tf_op jit(solution)/shard_map/all_gather | solution.py:24
  623.7 1.1 reshape.39
  624.8 0.3 fusion.14
  625.1 0.1 copy.19
  625.2 0.1 copy.20
  625.3 0.1 copy.18
  625.4 0.1 copy.21
  625.6 11.6 select_reduce_fusion.3
  637.2 348.3 %psum.42 = f32[512,4]{0,1:T(4,128)S(1)} all-reduce(f32[512,4]{0,1:T(4,128)S(1)} %pad_maximum_fusion), channel_id=1, replica_groups=mesh['slab'=32,'col'=4,'pb'=2] {'slab','col'}, use_global_device_ids=true, to_apply=%region_4.5 | all-reduce | flops 2048 | bytes 16384 | tf_op jit(solution)/shard_map/psum | solution.py:37
  985.5 17.1 fusion.1
  1002.7 681.8 %all-reduce = (f32[512]{0:T(512)S(1)}, f32[512,4]{0,1:T(4,128)S(1)}) all-reduce(f32[512]{0:T(512)S(1)} %add_multiply_fusion, f32[512,4]{0,1:T(4,128)S(1)} %maximum_multiply_fusion), channel_id=1, replica_groups=mesh['slab'=32,'col'=4,'pb'=2] {'slab','col'}, use_global_device_ids=true, to_apply=%region_9.10 | all-reduce | flops 2560 | bytes 20480 | tf_op jit(solution)/shard_map/psum | solution.py:48
  1684.5 0.0 copy-start.1
  1684.5 21.1 fusion.4
  1705.6 0.0 all-reduce.5.cloned.1.call-update
  1705.7 0.0 all-reduce.7.cloned.1.call-start
  1705.7 291.5 %all-reduce.5.cloned.1.call-done = f32[512,768]{1,0:T(8,128)} async-done(((f32[512,768]{1,0:T(8,128)}), f32[512,768]{1,0:T(8,128)}) %all-reduce.5.cloned.1.call-update) | async-done | bytes 1572880 | tf_op jit(solution)/shard_map/psum | solution.py:54
  1997.2 0.0 copy-done.1
  1997.2 4.2 convolution_bitcast_fusion
  2001.4 0.0 all-reduce.7.cloned.1.call-update
  2001.4 0.0 all-reduce.9.cloned.1.call-start
  2001.5 151.1 %all-reduce.7.cloned.1.call-done = f32[768,768]{0,1:T(8,128)} async-done(((f32[768,768]{0,1:T(8,128)}), f32[768,768]{0,1:T(8,128)}) %all-reduce.7.cloned.1.call-update) | async-done | bytes 2359312 | tf_op jit(solution)/shard_map/psum | solution.py:11
  2152.5 0.0 all-reduce.9.cloned.1.call-update
  2152.6 0.6 dynamic_slice.6
  2153.2 3.4 fusion.7
  2156.5 68.8 %all-reduce.9.cloned.1.call-done = f32[768,768]{0,1:T(8,128)} async-done(((f32[768,768]{0,1:T(8,128)}), f32[768,768]{0,1:T(8,128)}) %all-reduce.9.cloned.1.call-update) | async-done | bytes 2359312 | tf_op jit(solution)/shard_map/psum | solution.py:11
  2225.3 3.0 copy.17
  (10 shorter events, 0.1 us)
Async XLA Ops:
  7.2 309.0 %copy-start = (f32[768,768]{1,0:T(8,128)S(1)}, f32[768,768]{1,0:T(8,128)}, u32[]{:S(2)}) copy-start(f32[768,768]{1,0:T(8,128)} %param.5) | copy-start | bytes 7077892
  7.2 1990.0 %all-reduce.5.cloned.1.call-start = ((), (), s32[]{:S(2)}) async-start(), calls=%async_computation | async-start | bytes 3145728 | tf_op jit(solution)/shard_map/psum | solution.py:54
  1684.5 312.7 %copy-start.1 = (f32[4,768]{1,0:T(4,128)S(1)}, f32[4,768]{1,0:T(4,128)}, u32[]{:S(2)}) copy-start(f32[4,768]{1,0:T(4,128)} %param.4) | copy-start | bytes 36868
  1705.7 446.9 %all-reduce.7.cloned.1.call-start = ((), (), s32[]{:S(2)}) async-start(), calls=%async_computation.1 | async-start | bytes 4718592 | tf_op jit(solution)/shard_map/psum | solution.py:11
  2001.4 223.9 %all-reduce.9.cloned.1.call-start = ((), (), s32[]{:S(2)}) async-start(), calls=%async_computation.2 | async-start | bytes 4718592 | tf_op jit(solution)/shard_map/psum | solution.py:11
Sparse Core Ops, SparseCore 0:
  1705.8 291.3 all-reduce.4
  2001.7 150.7 all-reduce.6
  2154.9 70.3 all-reduce.8

commit v2 on v0

--- a/solution.py
+++ b/solution.py
@@ -1,9 +1,19 @@
+import functools
 import jax
 import jax.numpy as jnp
 from jax import lax
 from jax.sharding import PartitionSpec as P
 
 POS = 4
+
+
+def register_view(local_array, mesh_name, axis_name):
+    for src_i in (mesh_name, axis_name):
+        local_array = lax.psum(local_array, axis_name=src_i)
+    return local_array
+
+
+set_side_on_mesh = functools.partial(register_view, mesh_name="col", axis_name="slab")
 
 
 def shards(queries_raw, projection, passages, positives):
@@ -39,7 +49,7 @@
         slope_sum = slope_sum + slope
         pos_list.append(-jnp.sum(slope, axis=1))
     pos_part = jnp.stack(pos_list, axis=1) * scale
-    pos_grad, loss_total = lax.psum((pos_part, loss_part * scale), ("slab", "col"))
+    pos_grad, loss_total = set_side_on_mesh((pos_part, loss_part * scale))
     grad = slope_sum * scale
     for slot in range(POS):
         grad = grad + jnp.where(owned[slot], pos_grad[:, slot : slot + 1], 0.0)

time: 2270 us -> 1740 us (0.77)
  blocking collectives: 1640 us -> 1180 us
  waiting for transfers between devices: 549 us -> 485 us
    psum x1 -> x2, blocking collectives: 682 us -> 218 us  [register_view(): local_array = lax.psum(local_array, axis_name=src_i)]
    psum x1, waiting for transfers between devices: 291 us -> 227 us  [shards(): lax.psum(jnp.dot(grad_b, passages, preferred_element_type=jnp.float32), (...]
where the time goes in v2:
time: 1740 us
  blocking collectives  1180 us (68%)
  waiting for transfers between devices  485 us (28%)
  matrix products  42.2 us (2%)
    psum x1, blocking collectives, shards(): pos_scores = lax.psum(partial_pos, ('slab', 'col'))  348 us
    all_gather x1, blocking collectives, shards(): lax.all_gather(positives, ('slab', 'col'), axis=0, tiled=True)  309 us
    all_gather x1, blocking collectives, shards(): lax.all_gather(query_emb, ('slab', 'col'), axis=0, tiled=True)  306 us
    psum x1, waiting for transfers between devices, shards(): grad_projection = lax.psum(term, ('slab', 'col', 'pb'))  257 us
    psum x1, waiting for transfers between devices, shards(): lax.psum(jnp.dot(grad_b, passages, preferred_element_type=jnp.float32), (...  227 us
    psum x2, blocking collectives, register_view(): local_array = lax.psum(local_array, axis_name=src_i)  218 us
  transfers between devices with their start and end apart: 2, of which 2 were waited for; matrix products, arithmetic and copies ran while one was open for 0% of the time, Pallas kernels for 0%

profile of v2, /device:TPU:2, one launch (start us, length us, event | category | flops | bytes accessed | tf_op | source)
XLA Modules:
  0.0 1744.2 jit_solution(11891850312172584024)
XLA Ops:
  7.2 0.0 copy-start
  7.2 0.0 all-reduce.5.cloned.1.call-start
  7.2 309.0 %all-gather.1 = s32[128,4,4]{2,1,0:T(4,128)S(1)} all-gather(s32[1,4,4]{2,1,0:T(4,128)} %bitcast.45), channel_id=1, replica_groups=mesh['slab'=32,'col'=4,'pb'=2] {'slab','col'}, dimensions={0}, use_global_device_ids=true | all-gather | bytes 8256 | tf_op jit(solution)/shard_map/all_gather | solution.py:29
  316.2 0.0 copy-done
  316.2 1.9 fusion.5
  318.1 305.6 %all-gather = bf16[128,4,768]{2,1,0:T(4,128)(2,1)S(1)} all-gather(bf16[1,4,768]{2,1,0:T(4,128)(2,1)S(1)} %fusion.5), channel_id=1, replica_groups=mesh['slab'=32,'col'=4,'pb'=2] {'slab','col'}, dimensions={0}, use_global_device_ids=true | all-gather | bytes 792576 | tf_op jit(solution)/shard_map/all_gather | solution.py:28
  623.7 1.1 reshape.39
  624.8 0.3 fusion.14
  625.1 0.1 copy.19
  625.2 0.1 copy.20
  625.3 0.1 copy.18
  625.4 0.1 copy.21
  625.6 11.6 select_reduce_fusion.3
  637.2 348.3 %psum.49 = f32[512,4]{0,1:T(4,128)S(1)} all-reduce(f32[512,4]{0,1:T(4,128)S(1)} %pad_maximum_fusion), channel_id=1, replica_groups=mesh['slab'=32,'col'=4,'pb'=2] {'slab','col'}, use_global_device_ids=true, to_apply=%region_4.5 | all-reduce | flops 2048 | bytes 16384 | tf_op jit(solution)/shard_map/psum | solution.py:41
  985.5 17.1 fusion.1
  1002.7 14.3 all-reduce.1
  1017.0 203.3 %all-reduce = (f32[512]{0:T(512)S(1)}, f32[512,4]{0,1:T(4,128)S(1)}) all-reduce(f32[512]{0:T(512)S(1)} %get-tuple-element.26, f32[512,4]{0,1:T(4,128)S(1)} %get-tuple-element.27), channel_id=1, replica_groups=mesh['slab'=32,'col'=4,'pb'=2] {'slab'}, use_global_device_ids=true, to_apply=%region_10.11 | all-reduce | flops 2560 | bytes 20480 | tf_op jit(solution)/shard_map/psum | solution.py:12
  1220.3 0.0 copy-start.1
  1220.4 21.1 %fusion.4 = f32[512,768]{1,0:T(8,128)} fusion(bf16[4096,768]{1,0:T(8,128)(2,1)} %param.6, f32[512,4096]{1,0:T(8,128)} %get-tuple-element.34, f32[512,4096]{1,0:T(8,128)} %get-tuple-element.28, f32[512,4096]{1,0:T(8,128)} %get-tuple-element.40, f32[512,4096]{1,0:T(8,128)} %get-tuple-element.37, f32[512]{0:T(512)S(1)} %bitcast.55, f32[512]{0:T(512)S(1)} %bitcast.56, ...), kind=kOutput, calls=%fused_computation.21 | convolution fusion | flops 3273654272 | bytes 41435136 | tf_op jit(solution)/shard_map/dot_general | solution.py:59
  1241.4 0.0 all-reduce.5.cloned.1.call-update
  1241.5 0.0 all-reduce.7.cloned.1.call-start
  1241.5 227.2 %all-reduce.5.cloned.1.call-done = f32[512,768]{1,0:T(8,128)} async-done(((f32[512,768]{1,0:T(8,128)}), f32[512,768]{1,0:T(8,128)}) %all-reduce.5.cloned.1.call-update) | async-done | bytes 1572880 | tf_op jit(solution)/shard_map/psum | solution.py:58
  1468.7 0.0 copy-done.1
  1468.7 4.2 convolution_bitcast_fusion
  1472.9 0.0 all-reduce.7.cloned.1.call-update
  1472.9 0.6 dynamic_slice.6
  1473.5 3.4 fusion.7
  1476.9 257.4 %all-reduce.7.cloned.1.call-done = f32[768,768]{0,1:T(8,128)} async-done(((f32[768,768]{0,1:T(8,128)}), f32[768,768]{0,1:T(8,128)}) %all-reduce.7.cloned.1.call-update) | async-done | bytes 2359312 | tf_op jit(solution)/shard_map/psum | solution.py:65
  1734.3 3.0 copy.17
  (10 shorter events, 0.1 us)
Async XLA Ops:
  7.2 309.0 %copy-start = (f32[768,768]{1,0:T(8,128)S(1)}, f32[768,768]{1,0:T(8,128)}, u32[]{:S(2)}) copy-start(f32[768,768]{1,0:T(8,128)} %param.5) | copy-start | bytes 7077892
  7.2 1461.5 %all-reduce.5.cloned.1.call-start = ((), (), s32[]{:S(2)}) async-start(), calls=%async_computation | async-start | bytes 3145728 | tf_op jit(solution)/shard_map/psum | solution.py:58
  1220.3 248.4 %copy-start.1 = (f32[4,768]{1,0:T(4,128)S(1)}, f32[4,768]{1,0:T(4,128)}, u32[]{:S(2)}) copy-start(f32[4,768]{1,0:T(4,128)} %param.4) | copy-start | bytes 36868
  1241.5 492.8 %all-reduce.7.cloned.1.call-start = ((), (), s32[]{:S(2)}) async-start(), calls=%async_computation.1 | async-start | bytes 4718592 | tf_op jit(solution)/shard_map/psum | solution.py:65
Sparse Core Ops, SparseCore 0:
  1241.6 227.0 all-reduce.4
  1475.6 258.6 all-reduce.6
